TPU v7x, 256 devices: a whole 4x4x8 slice. The times are simulated.
256 devices in a mesh: rep: 8 (over z_hi, y), tp: 32 (over x, z_lo, core).
Axes of the slice: x: 4, y: 4, z: 8 (z_hi: 2, z_lo: 4; z = z_hi * 4 + z_lo), core: 2. Of those that a mesh axis runs over, the one named last changes fastest.
Arguments:
- prompts: bfloat16 [32, 96, 8192], P('rep', None, 'tp'), may hold values from -6 to 6
- output_matrix: bfloat16 [8192, 8192], P('tp'), may hold values from -0.125 to 0.125
- adapter_weight_pair: bfloat16 [32, 8192, 128], P('tp'), may hold values from -0.1875 to 0.1875
- adapter: int32 [32], replicated, may hold values from 0 to 31
- lengths: int32 [32], replicated, may hold values from 1 to 96, 2304 in all
- placement: int32 [32, 1], replicated, may hold values from 0 to 7; in each aligned block of 4 rows (0 to 3, 4 to 7, ...) no two rows name the same one
Outputs:
- served: bfloat16 [8, 8, 96, 8192], P('rep', None, None, 'tp')
Inputs may be any that keep to these rules, and one draw needn't show every extreme that they name: `placement`: among the 4 prompts of one index of rep, no group is named more than 1 times, a bound that some block reaches. `lengths`: the largest length equals 96.
All inputs are finite; a program needn't handle non-finite values.
Results may differ from a plain program's by a relative error of at most 0.0034.
Values may be sent and summed in bfloat16 or wider, within the bound.
A program may use at most 128 MiB of HBM per device.

v0:
```python
import jax
import jax.numpy as jnp
from jax import lax
from jax.sharding import PartitionSpec as P


def local(prompts, output_matrix, adapter_weight_pair, adapter, lengths, placement):
    groups = lax.axis_size("rep")
    my_group = lax.axis_index("rep")
    per_group = prompts.shape[0]
    row_count = prompts.shape[1]
    send_cap = max(1, 2 * per_group // groups)
    slot_count = groups * send_cap
    prompt_count = adapter.shape[0]
    rank_columns = adapter_weight_pair.shape[2] // 2
    adapter_library = lax.all_to_all(
        adapter_weight_pair, "tp", split_axis=1, concat_axis=0, tiled=True
    )
    prompt_ids = jnp.arange(prompt_count, dtype=jnp.int32)
    home_group = prompt_ids // per_group
    target = placement[:, 0]
    earlier = (
        (home_group[:, None] == home_group[None, :])
        & (target[:, None] == target[None, :])
        & (prompt_ids[None, :] < prompt_ids[:, None])
    )
    order_rank = jnp.sum(earlier.astype(jnp.int32), axis=1)
    slot_index = home_group * send_cap + order_rank
    send_index = target * send_cap + order_rank
    local_send = lax.dynamic_slice_in_dim(send_index, my_group * per_group, per_group)
    slot_ids = jnp.arange(slot_count, dtype=jnp.int32)
    selector = (slot_ids[:, None] == local_send[None, :]).astype(jnp.bfloat16)
    row_ids = jnp.arange(row_count, dtype=jnp.int32)
    bank_ids = jnp.arange(adapter_library.shape[0], dtype=jnp.int32)
    received = lax.all_to_all(
        jnp.einsum("sj,jrf->srf", selector, prompts, preferred_element_type=jnp.float32).astype(
            jnp.bfloat16
        ),
        "rep",
        split_axis=0,
        concat_axis=0,
        tiled=True,
    )
    slot_match = (
        (target[None, :] == my_group) & (slot_index[None, :] == slot_ids[:, None])
    ).astype(jnp.int32)
    slot_adapters = jnp.sum(slot_match * adapter[None, :], axis=1)
    slot_lengths = jnp.sum(slot_match * lengths[None, :], axis=1)
    item_count = received.shape[0]
    partial_value = jnp.dot(
        received.reshape(item_count * row_count, received.shape[2]),
        output_matrix,
        preferred_element_type=jnp.float32,
    )
    base_sum = lax.psum_scatter(partial_value, "tp", scatter_dimension=1, tiled=True)
    onehot = (slot_adapters[:, None] == bank_ids[None, :]).astype(jnp.bfloat16)
    picked_adapter = jnp.einsum(
        "sa,afk->sfk", onehot, adapter_library, preferred_element_type=jnp.float32
    ).astype(jnp.bfloat16)
    down_part = jnp.einsum(
        "srf,sfk->srk",
        received,
        picked_adapter[:, :, :rank_columns],
        preferred_element_type=jnp.float32,
    )
    down_sum = lax.psum(down_part, "tp").astype(jnp.bfloat16)
    lifted = jnp.einsum(
        "srk,sfk->srf",
        down_sum,
        picked_adapter[:, :, rank_columns:],
        preferred_element_type=jnp.float32,
    )
    live_rows = (row_ids[None, :] < slot_lengths[:, None]).astype(jnp.float32)
    result = (
        (base_sum.reshape(item_count, row_count, -1) + 0.5 * lifted) * live_rows[:, :, None]
    ).astype(jnp.bfloat16)
    return result[None]


def solution(mesh):
    in_specs = (P("rep", None, "tp"), P("tp", None), P("tp", None, None), P(), P(), P())
    out_specs = P("rep", None, None, "tp")
    return jax.shard_map(local, mesh=mesh, in_specs=in_specs, out_specs=out_specs, check_vma=False)
```

profile of v0, /device:TPU:32, one launch (start us, length us, event | category | flops | bytes accessed | tf_op | source)
XLA Modules:
  0.0 383.5 jit_solution(9808151408638049542)
XLA Ops:
  6.5 0.9 convert_reduce_fusion
  7.5 0.7 fusion.23
  8.1 0.1 dynamic_slice.3
  8.2 0.4 convolution_convert_fusion
  8.6 0.1 copy.20
  8.7 26.8 %all_to_all.17 = bf16[8,96,256]{2,1,0:T(8,128)(2,1)S(1)} all-to-all(bf16[8,96,256]{2,1,0:T(8,128)(2,1)S(1)} %copy.20), channel_id=1, replica_groups=mesh['rep'=8,'tp'=32] {'rep'}, dimensions={0} | all-to-all | bytes 786432 | tf_op jit(solution)/shard_map/all_to_all | solution.py:35
  35.4 12.2 %fusion.25 = f32[768,8192]{1,0:T(8,128)} fusion(bf16[768,256]{1,0:T(8,128)(2,1)S(1)} %bitcast.25, bf16[256,8192]{1,0:T(8,128)(2,1)} %param.7), kind=kOutput, calls=%fused_computation.38 | convolution fusion | flops 3221225472 | bytes 29753344 | tf_op jit(solution)/shard_map/dot_general | solution.py:50
  47.7 0.0 reduce-scatter.2.cloned.1.call-update
  47.7 1.6 copy-done.1
  49.3 33.2 %copy.37 = bf16[1,8192,128]{2,0,1:T(2,128)(2,1)} copy(bf16[1,8192,128]{2,1,0:T(8,128)(2,1)S(1)} %copy-done.1) | data formatting | bytes 4194304 | tf_op args[2]
  82.5 0.5 broadcast.102
  83.0 45.2 %reduce = bf16[8192,128]{1,0:T(8,128)(2,1)S(1)} reduce(bf16[8192,1,128]{2,1,0:T(2,128)(2,1)} %bitcast.22, bf16[]{:T(256)} %broadcast.102), dimensions={1}, to_apply=%bitcast.21.reduce_sub_computation | reduce | bytes 4194306
  128.2 2.1 reshape.78
  130.3 6.5 %all-to-all-start.1 = ((bf16[32,2,16384]{2,1,0:T(2,128)(2,1)}), bf16[32,2,16384]{2,1,0:T(2,128)(2,1)S(1)}, u32[]{:S(2)}, u32[]{:S(2)}) async-start(bf16[32,2,16384]{2,1,0:T(2,128)(2,1)} %reshape.78), calls=%async_computation.2 | async-start | bytes 4194304 | tf_op jit(solution)/shard_map/all_to_all | solution.py:16
  136.9 0.1 select_reduce_fusion
  137.0 0.1 fusion.18
  137.1 82.1 %all-to-all-done.1 = bf16[32,2,16384]{2,1,0:T(2,128)(2,1)S(1)} async-done(((bf16[32,2,16384]{2,1,0:T(2,128)(2,1)}), bf16[32,2,16384]{2,1,0:T(2,128)(2,1)S(1)}, u32[]{:S(2)}, u32[]{:S(2)}) %all-to-all-start.1) | async-done | bytes 2097184 | tf_op jit(solution)/shard_map/all_to_all | solution.py:16
  219.3 6.8 %reshape.79 = bf16[8192,1,128]{2,1,0:T(2,128)(2,1)} reshape(bf16[32,2,16384]{2,1,0:T(2,128)(2,1)S(1)} %all-to-all-done.1) | data formatting | bytes 4194304
  226.1 2.5 copy.25
  228.6 1.2 fusion.2
  229.8 0.2 fusion.24
  230.1 0.3 fusion.10
  230.4 144.1 %all-reduce.1 = bf16[8,96,64]{1,2,0:T(8,128)(2,1)S(1)} all-reduce(f32[8,96,64]{1,2,0:T(8,128)S(1)} %fusion.10), channel_id=1, replica_groups=mesh['rep'=8,'tp'=32] {'tp'}, use_global_device_ids=true, to_apply=%region_3.4 | all-reduce | flops 49152 | bytes 294912 | tf_op jit(solution)/shard_map/psum | solution.py:66
  374.5 2.2 fusion.8
  (13 shorter events, 0.0 us)
Async XLA Ops:
  6.5 1.7 copy-start
  6.5 367.9 %reduce-scatter.2.cloned.1.call-start = ((), (), s32[]{:S(2)}) async-start(), calls=%async_computation.3 | async-start | bytes 25952256 | tf_op jit(solution)/shard_map/reduce_scatter | solution.py:55
  47.7 1.6 copy-start.1
  130.3 6.5 %copy-start.2 = (s32[32,1]{0,1:T(1,128)S(1)}, s32[32,1]{0,1:T(1,128)}, u32[]{:S(2)}) copy-start(s32[32,1]{0,1:T(1,128)} %param.11) | copy-start | bytes 388
  130.3 6.5 %copy-start.3 = (s32[32]{0:T(128)S(1)}, s32[32]{0:T(128)}, u32[]{:S(2)}) copy-start(s32[32]{0:T(128)} %param.10) | copy-start | bytes 388
  130.3 6.6 %copy-start.4 = (s32[32]{0:T(128)S(1)}, s32[32]{0:T(128)}, u32[]{:S(2)}) copy-start(s32[32]{0:T(128)} %param.9) | copy-start | bytes 388
  130.3 88.9 %all-to-all-start.1 = ((bf16[32,2,16384]{2,1,0:T(2,128)(2,1)}), bf16[32,2,16384]{2,1,0:T(2,128)(2,1)S(1)}, u32[]{:S(2)}, u32[]{:S(2)}) async-start(bf16[32,2,16384]{2,1,0:T(2,128)(2,1)} %reshape.78), calls=%async_computation.2 | async-start | bytes 4194304 | tf_op jit(solution)/shard_map/all_to_all | solution.py:16
Sparse Core Ops, SparseCore 0:
  47.8 318.7 reduce-scatter.1
where the time goes:
time: 388 us; the launch traced here: 384 us
  blocking collectives  171 us (44%)
  waiting for transfers between devices  82.2 us (21%)
  local copies, waits for them, and re-layouts  47.2 us (12%)
  other arithmetic  47 us (12%)
  matrix products  16.3 us (4%)
  between operations  13.5 us (3%)
  starting transfers between devices  6.51 us (2%)
    psum x1, blocking collectives, local(): down_sum = lax.psum(down_part, 'tp').astype(jnp.bfloat16)  144 us
    all_to_all x1, waiting for transfers between devices, local(): lax.all_to_all(adapter_weight_pair, 'tp', split_axis=1, concat_axis=0, ti...  82.1 us
    unnamed x15, local copies, waits for them, and re-layouts  46.8 us
    unnamed x1, other arithmetic  45.2 us
    all_to_all x1, blocking collectives, local(): lax.all_to_all(jnp.einsum('sj,jrf->srf', selector, prompts, preferred_ele...  26.8 us
    dot_general x1, matrix products, local(): jnp.dot(received.reshape(item_count * row_count, received.shape[2]), outp...  12.2 us
  transfers between devices with their start and end apart: 2, of which 1 were waited for; matrix products, arithmetic and copies ran while one was open for 24% of the time, Pallas kernels for 0%

commit v1 on v0

v1 whole, which is shorter than its diff:
```python
import functools

import jax
import jax.numpy as jnp
from jax import lax
from jax.experimental import pallas as pl
from jax.experimental.pallas import tpu as pltpu
from jax.sharding import PartitionSpec as P

MESH = pl.DeviceIdType.MESH
BF = jnp.bfloat16
F32 = jnp.float32

NX, NZ, NC = 4, 4, 2
NY, NH = 4, 2


def kernel(
    adapter_s, lengths_s, target_s, x_ref, w_ref, a_ref, out_ref,
    x_sib, w_own, w_sib,
    s_far, s_dir, s_acc, r_far, r_dir, r_acc,
    s_z, r_z, base,
    lib, s_sel, sel, dpack, r_sib, x_sum, z_sum, down, r_down,
    s_out,
    w_own_sem, w_send, w_recv, x_send, x_recv,
    far_send, far_recv, dir_send, dir_recv, acc_send, acc_recv,
    z_send, z_recv,
    lib_own, lib_send, lib_recv, sel_send, sel_recv,
    down_send, down_recv, out_send, out_recv,
):
    rep = lax.axis_index("rep")
    tp = lax.axis_index("tp")
    hi, y = rep // NY, rep % NY
    x = tp // (NZ * NC)
    zl = (tp // NC) % NZ
    core = tp % NC
    tps, reps = NX * NZ * NC, NY * NH
    prompts, rows = out_ref.shape[0] // 2, out_ref.shape[1]
    width = out_ref.shape[2]
    share = width // NY

    def tp_of(xx, zz, cc):
        return (xx * NZ + zz) * NC + cc

    def copy(src, dst, send, recv, r=None, t=None):
        return pltpu.make_async_remote_copy(
            src_ref=src, dst_ref=dst, send_sem=send, recv_sem=recv,
            device_id=(rep if r is None else r, tp if t is None else t),
            device_id_type=MESH,
        )

    sib = tp_of(x, zl, 1 - core)

    barrier = pltpu.get_barrier_semaphore()

    @pl.loop(1, tps)
    def _(j):
        pl.semaphore_signal(barrier, inc=1, device_id=(rep, (tp + j) % tps), device_id_type=MESH)

    @pl.loop(1, reps)
    def _(j):
        pl.semaphore_signal(barrier, inc=1, device_id=((rep + j) % reps, tp), device_id_type=MESH)

    def w_columns(d, q, cc):
        start = tp_of((x + d) % NX, q, cc) * width
        return w_ref.at[:, pl.ds(pl.multiple_of(start, width), width)]

    order = (2, 1, 3, 0)
    pairs = (0, 3, 1, 2)
    own_copies = {}
    for d in order:
        for q in pairs:
            own_copies[d, q] = pltpu.make_async_copy(
                w_columns(d, q, core), w_own.at[d, q], w_own_sem.at[d, q]
            )
            own_copies[d, q].start()
    lib_copy = pltpu.make_async_copy(
        a_ref.at[pl.ds(pl.multiple_of(tp * width + y * share, share), share), :], lib.at[tp], lib_own
    )
    lib_copy.start()

    pl.semaphore_wait(barrier, tps - 1 + reps - 1)

    x_copy = copy(x_ref, x_sib, x_send, x_recv, t=sib)
    x_copy.start()
    w_copies = {}
    for d in order:
        for q in pairs:
            w_copies[d, q] = copy(
                w_columns(d, q, 1 - core), w_sib.at[d, q], w_send.at[d, q], w_recv.at[d, q], t=sib
            )
            w_copies[d, q].start()

    @pl.loop(1, tps)
    def _(j):
        to = (tp + j) % tps
        copy(
            a_ref.at[pl.ds(pl.multiple_of(to * width + y * share, share), share), :],
            lib.at[tp], lib_send, lib_recv, t=to,
        ).start()

    ready = set()

    def partial(d, q):
        if not ready:
            x_copy.wait_recv()
        if (d, q) not in ready:
            own_copies[d, q].wait()
            w_copies[d, q].wait_recv()
            ready.add((d, q))
        return jnp.dot(x_ref[...], w_own[d, q], preferred_element_type=F32) + jnp.dot(
            x_sib[...], w_sib[d, q], preferred_element_type=F32
        )

    def way(q):
        return 1 if q < NZ // 2 else 3

    fars, dirs, accs, zs = {}, {}, {}, {}

    def far_step(q):
        s_far[q] = partial(2, q).astype(BF)
        fars[q] = copy(
            s_far.at[q], r_far.at[q], far_send.at[q], far_recv.at[q],
            t=tp_of((x + way(q)) % NX, zl, core),
        )
        fars[q].start()

    def dir_step(q):
        d = NX - way(q)
        s_dir[q] = partial(d, q).astype(BF)
        dirs[q] = copy(
            s_dir.at[q], r_dir.at[q], dir_send.at[q], dir_recv.at[q],
            t=tp_of((x + d) % NX, zl, core),
        )
        dirs[q].start()

    def acc_step(q):
        d = way(q)
        own = partial(d, q)
        fars[q].wait_recv()
        s_acc[q] = (own + r_far[q].astype(F32)).astype(BF)
        accs[q] = copy(
            s_acc.at[q], r_acc.at[q], acc_send.at[q], acc_recv.at[q],
            t=tp_of((x + d) % NX, zl, core),
        )
        accs[q].start()

    def z_step(q):
        own = partial(0, q)
        dirs[q].wait_recv()
        accs[q].wait_recv()
        total = own + r_dir[q].astype(F32) + r_acc[q].astype(F32)

        @pl.when(q == zl)
        def _():
            base[...] = total

        zs[q] = copy(
            s_z.at[q], r_z.at[zl], z_send.at[q], z_recv.at[zl], t=tp_of(x, q, core)
        )

        @pl.when(q != zl)
        def _():
            s_z[q] = total.astype(BF)
            zs[q].start()

    for q in (0, 3):
        far_step(q)
    for q in (0, 3):
        dir_step(q)
    for q in (0, 3):
        acc_step(q)
    for q in (1, 2):
        far_step(q)
    for q in (1, 2):
        dir_step(q)

    lib_copy.wait()
    lib_all = copy(
        lib.at[pl.ds(0, tps - 1)], lib.at[pl.ds(0, tps - 1)], lib_send, lib_recv, t=sib
    )
    lib_all.wait_recv()
    sels = []
    for j in range(1, NY):
        to = hi * NY + (y + j) % NY
        for p in range(prompts):
            s_sel[j, p] = lib[adapter_s[to * prompts + p]]
        sels.append(copy(
            s_sel.at[j], sel.at[:, y], sel_send.at[j], sel_recv.at[y], r=to
        ))
        sels[-1].start()
    for p in range(prompts):
        sel[p, y] = lib[adapter_s[rep * prompts + p]]

    for q in (0, 3):
        z_step(q)

    for j in range(1, NY):
        fr = (y + j) % NY
        copy(s_sel.at[j], sel.at[:, fr], sel_send.at[j], sel_recv.at[fr], r=hi * NY + fr).wait_recv()

    def chosen(p):
        return sel[p].reshape(width, sel.shape[3])

    rank = sel.shape[3] // 2
    for k in range(2):
        parts = [
            jnp.dot(
                x_ref[pl.ds((2 * k + i) * rows, rows), :], chosen(2 * k + i),
                preferred_element_type=F32,
            )
            for i in range(2)
        ]
        dpack[k] = jnp.concatenate([parts[0][:, :rank], parts[1][:, :rank]], axis=1)
    sib_copy = copy(dpack.at[1 - core], r_sib, down_send.at[0], down_recv.at[0], t=sib)
    sib_copy.start()

    for q in (1, 2):
        acc_step(q)

    sib_copy.wait_recv()
    x_sum[x] = dpack[core] + r_sib[...]
    d_copies = []
    for j in range(1, NX):
        c = copy(
            x_sum.at[x], x_sum.at[x], down_send.at[j], down_recv.at[1 + x],
            t=tp_of((x + j) % NX, zl, core),
        )
        c.start()
        d_copies.append(c)
    for j in range(1, NX):
        fr = (x + j) % NX
        copy(
            x_sum.at[fr], x_sum.at[fr], down_send.at[j], down_recv.at[1 + fr],
            t=tp_of(fr, zl, core),
        ).wait_recv()
    z_sum[zl] = (x_sum[0] + x_sum[1]) + (x_sum[2] + x_sum[3])
    for j in range(1, NZ):
        c = copy(
            z_sum.at[zl], z_sum.at[zl], down_send.at[NX - 1 + j], down_recv.at[1 + NX + zl],
            t=tp_of(x, (zl + j) % NZ, core),
        )
        c.start()
        d_copies.append(c)

    for q in (1, 2):
        z_step(q)

    for j in range(1, NZ):
        fr = (zl + j) % NZ
        copy(
            z_sum.at[fr], z_sum.at[fr], down_send.at[NX - 1 + j], down_recv.at[1 + NX + fr],
            t=tp_of(x, fr, core),
        ).wait_recv()
    down[...] = ((z_sum[0] + z_sum[1]) + (z_sum[2] + z_sum[3])).astype(BF)
    back = copy(down, r_down, down_send.at[NX + NZ - 1], down_recv.at[1 + NX + NZ], t=sib)
    back.start()
    back.wait_recv()

    mine, other = down[...], r_down[...]
    packs = [jnp.where(core == 0, mine, other), jnp.where(core == 0, other, mine)]
    lanes = lax.broadcasted_iota(jnp.int32, (rows, 2 * rank), 1)
    row_ids = lax.broadcasted_iota(jnp.int32, (rows, width), 0)
    lifted = []
    for p in range(prompts):
        pack = packs[p // 2].astype(F32)
        if p % 2 == 0:
            pack = jnp.concatenate([pack[:, rank:], pack[:, :rank]], axis=1)
        pack = jnp.where(lanes >= rank, pack, 0.0).astype(BF)
        lifted.append(0.5 * lax.dot_general(
            pack, chosen(p), (((1,), (1,)), ((), ())), preferred_element_type=F32
        ))

    for j in range(1, NZ):
        fr = (zl + j) % NZ
        copy(
            s_z.at[0], r_z.at[fr], z_send.at[0], z_recv.at[fr], t=tp_of(x, fr, core)
        ).wait_recv()
    results = []
    for p in range(prompts):
        span = pl.ds(p * rows, rows)
        total = base[span, :] + lifted[p]
        for j in range(1, NZ):
            total += r_z[(zl + j) % NZ, span, :].astype(F32)
        live = row_ids < lengths_s[rep * prompts + p]
        results.append(jnp.where(live, total, 0.0))

    outs = []
    for j in range(reps):
        to = (rep + j) % reps
        value = jnp.zeros((rows, width), F32)
        for p in range(prompts):
            value = jnp.where(target_s[rep * prompts + p] == to, results[p], value)
        if j == 0:
            out_ref[rep] = value.astype(BF)
        else:
            s_out[j] = value.astype(BF)
            outs.append(copy(
                s_out.at[j], out_ref.at[rep], out_send.at[j], out_recv.at[rep], r=to
            ))
            outs[-1].start()

    x_copy.wait_send()
    for c in w_copies.values():
        c.wait_send()
    lib_all.wait_send()
    for group in (fars, dirs, accs):
        for c in group.values():
            c.wait_send()
    for q in range(NZ):
        @pl.when(q != zl)
        def _(q=q):
            zs[q].wait_send()
    for c in sels + [sib_copy, back] + d_copies + outs:
        c.wait_send()
    for j in range(1, reps):
        fr = (rep + j) % reps
        copy(s_out.at[j], out_ref.at[fr], out_send.at[j], out_recv.at[fr], r=fr).wait_recv()


def local(prompts, output_matrix, adapter_weight_pair, adapter, lengths, placement):
    count, rows, width = prompts.shape
    reps = lax.axis_size("rep")
    tps = lax.axis_size("tp")
    pair = adapter_weight_pair.shape[2]
    tall = count * rows
    dma = pltpu.SemaphoreType.DMA
    smem = pl.BlockSpec(memory_space=pltpu.SMEM)
    vmem = pl.BlockSpec(memory_space=pltpu.VMEM)
    hbm = pl.BlockSpec(memory_space=pl.ANY)
    block = pltpu.VMEM((NZ, tall, width), BF)
    out = pl.pallas_call(
        kernel,
        out_shape=jax.ShapeDtypeStruct((reps, rows, width), BF),
        in_specs=[smem, smem, smem, vmem, hbm, hbm],
        out_specs=vmem,
        scratch_shapes=[
            pltpu.VMEM((tall, width), BF),
            pltpu.VMEM((NX, NZ, width, width), BF),
            pltpu.VMEM((NX, NZ, width, width), BF),
            block, block, block, block, block, block,
            block, block, pltpu.VMEM((tall, width), F32),
            pltpu.VMEM((tps, width // NY, pair), BF),
            pltpu.VMEM((NY, count, width // NY, pair), BF),
            pltpu.VMEM((count, NY, width // NY, pair), BF),
            pltpu.VMEM((2, rows, pair), F32),
            pltpu.VMEM((rows, pair), F32),
            pltpu.VMEM((NX, rows, pair), F32),
            pltpu.VMEM((NZ, rows, pair), F32),
            pltpu.VMEM((rows, pair), BF),
            pltpu.VMEM((rows, pair), BF),
            pltpu.VMEM((reps, rows, width), BF),
            dma((NX, NZ)), dma((NX, NZ)), dma((NX, NZ)), dma, dma,
            dma((NZ,)), dma((NZ,)), dma((NZ,)), dma((NZ,)), dma((NZ,)), dma((NZ,)),
            dma((NZ,)), dma((NZ,)),
            dma, dma, dma, dma((NY,)), dma((NY,)),
            dma((NX + NZ,)), dma((2 + NX + NZ,)), dma((reps,)), dma((reps,)),
        ],
        compiler_params=pltpu.CompilerParams(
            collective_id=0, has_side_effects=True, vmem_limit_bytes=48 * 1024 * 1024
        ),
    )(
        adapter, lengths, placement.reshape(-1), prompts.reshape(tall, width), output_matrix,
        adapter_weight_pair.reshape(-1, pair),
    )
    return out[None]


def solution(mesh):
    in_specs = (P("rep", None, "tp"), P("tp", None), P("tp", None, None), P(), P(), P())
    out_specs = P("rep", None, None, "tp")
    return jax.shard_map(local, mesh=mesh, in_specs=in_specs, out_specs=out_specs, check_vma=False)
```

time: 388 us -> 78.1 us (0.20); the launches traced: 384 us -> 77.9 us
  blocking collectives: 171 us -> 0 us
  waiting for transfers between devices: 82.2 us -> 0 us
  Pallas kernels: 0 us -> 72.7 us
  other arithmetic: 47 us -> 0 us
  local copies, waits for them, and re-layouts: 47.2 us -> 5.23 us
  matrix products: 16.3 us -> 0 us
  between operations: 13.5 us -> 0.01 us
  starting transfers between devices: 6.51 us -> 0 us
    psum x1 -> x0, blocking collectives: 144 us -> none  [local(): down_sum = lax.psum(down_part, 'tp').astype(jnp.bfloat16)]
    all_to_all x1 -> x0, waiting for transfers between devices: 82.1 us -> none  [local(): lax.all_to_all(adapter_weight_pair, 'tp', split_axis=1, concat_axis=0, ti...]
    pallas_call x0 -> x1, Pallas kernels: none -> 72.7 us  [local(): pl.pallas_call(kernel, out_shape=jax.ShapeDtypeStruct((reps, rows, width)...]
    unnamed x1 -> x0, other arithmetic: 45.2 us -> none
    unnamed x15 -> x11, local copies, waits for them, and re-layouts: 46.8 us -> 5.23 us
    all_to_all x1 -> x0, blocking collectives: 26.8 us -> none  [local(): lax.all_to_all(jnp.einsum('sj,jrf->srf', selector, prompts, preferred_ele...]
    dot_general x5 -> x0, matrix products: 16.3 us -> none  [the longest x1 12.2 us: local(): jnp.dot(received.reshape(item_count * row_count, received.shape[2]), outp...]
    all_to_all x1 -> x0, starting transfers between devices: 6.51 us -> none  [local(): lax.all_to_all(adapter_weight_pair, 'tp', split_axis=1, concat_axis=0, ti...]
  transfers between devices with their start and end apart: 2 -> 0, of which waited for: 1 -> 0; matrix products, arithmetic and copies ran while one was open for 24% -> 0% of each run, Pallas kernels for 0% -> 0%
where the time goes in v1:
time: 78.1 us; the launch traced here: 77.9 us
  Pallas kernels  72.7 us (93%)
  local copies, waits for them, and re-layouts  5.23 us (7%)
    pallas_call x1, Pallas kernels, local(): pl.pallas_call(kernel, out_shape=jax.ShapeDtypeStruct((reps, rows, width)...  72.7 us
    unnamed x11, local copies, waits for them, and re-layouts  5.23 us

profile of v1, /device:TPU:32, one launch (start us, length us, event | category | flops | bytes accessed | tf_op | source)
XLA Modules:
  0.0 77.9 jit_solution(4825254564829433392)
XLA Ops:
  0.0 0.0 copy-start
  0.0 1.6 %copy-done = bf16[1,8192,128]{2,1,0:T(8,128)(2,1)S(1)} copy-done((bf16[1,8192,128]{2,1,0:T(8,128)(2,1)S(1)}, bf16[1,8192,128]{2,1,0:T(8,128)(2,1)}, u32[]{:S(2)}) %copy-start) | copy-done | bytes 2097176
  1.6 0.0 copy-start.1
  1.6 0.9 %copy-done.1 = bf16[4,96,256]{2,1,0:T(8,128)(2,1)S(1)} copy-done((bf16[4,96,256]{2,1,0:T(8,128)(2,1)S(1)}, bf16[4,96,256]{2,1,0:T(8,128)(2,1)}, u32[]{:S(2)}) %copy-start.1) | copy-done | bytes 196632
  2.5 0.0 copy-start.2
  2.5 0.7 copy-done.2
  3.2 0.0 copy-start.3
  3.2 0.7 copy-done.3
  3.8 0.0 copy-start.4
  3.8 0.7 copy-done.4
  4.5 72.7 %shard_map.64 = bf16[8,96,256]{2,1,0:T(8,128)(2,1)S(1)} custom-call(s32[32]{0:T(128)S(1)} %copy-done.2, s32[32]{0:T(128)S(1)} %copy-done.3, s32[32]{0:T(128)S(1)} %bitcast.7, bf16[384,256]{1,0:T(8,128)(2,1)S(1)} %bitcast.6, bf16[256,8192]{1,0:T(8,128)(2,1)} %w_ref.1, bf16[8192,128]{1,0:T(8,128)(2,1)S(1)} %bitcast.4), custom_call_target="tpu_custom_call" | custom-call | tf_op jit(solution)/shard_map/pallas_call | solution.py:332
  77.2 0.7 copy.8
Async XLA Ops:
  0.0 1.6 %copy-start = (bf16[1,8192,128]{2,1,0:T(8,128)(2,1)S(1)}, bf16[1,8192,128]{2,1,0:T(8,128)(2,1)}, u32[]{:S(2)}) copy-start(bf16[1,8192,128]{2,1,0:T(8,128)(2,1)} %param.8) | copy-start | bytes 6291460
  1.6 0.9 %copy-start.1 = (bf16[4,96,256]{2,1,0:T(8,128)(2,1)S(1)}, bf16[4,96,256]{2,1,0:T(8,128)(2,1)}, u32[]{:S(2)}) copy-start(bf16[4,96,256]{2,1,0:T(8,128)(2,1)} %param.6) | copy-start | bytes 589828
  2.5 0.7 copy-start.2
  3.2 0.7 copy-start.3
  3.8 0.7 copy-start.4

commit v2 on v0

v2 whole, which is shorter than its diff:
```python
import functools

import jax
import jax.numpy as jnp
from jax import lax
from jax.experimental import pallas as pl
from jax.experimental.pallas import tpu as pltpu
from jax.sharding import PartitionSpec as P

MESH = pl.DeviceIdType.MESH
BF = jnp.bfloat16
F32 = jnp.float32

NX, NZ, NC = 4, 4, 2
NY, NH = 4, 2
FAR_FIRST = (6, 2, 5, 7, 4, 1, 3, 0)
SCHEDULE = (
    "W0", "lib", "F0", "W1", "W2", "W3", "D0", "C0", "F1", "D1", "S0", "C1", "choose", "F2",
    "D2", "S1", "C2", "down", "F3", "D3", "S2", "down_z", "C3", "S3", "down_back", "lift", "O0", "O1",
)


def kernel(
    adapter_h, lengths_h, target_h, x_hbm, w_ref, a_ref, out_ref,
    adapter_s, lengths_s, target_s, x_ref, x_sib, w_own, w_sib,
    s_far, s_dir, s_acc, r_far, r_dir, r_acc,
    s_z, r_z, base,
    lib, s_sel, sel, dpack, x_sum, z_sum, down, lifted,
    s_out,
    in_sem, w_own_sem, w_send, w_recv, x_send, x_recv,
    far_send, far_recv, dir_send, dir_recv, acc_send, acc_recv,
    z_send, z_recv,
    lib_own, lib_send, lib_recv, sel_send, sel_recv,
    down_send, down_recv, out_send, out_recv,
):
    rep = lax.axis_index("rep")
    tp = lax.axis_index("tp")
    hi, y = rep // NY, rep % NY
    x = tp // (NZ * NC)
    zl = (tp // NC) % NZ
    core = tp % NC
    tps, reps = NX * NZ * NC, NY * NH
    prompts, rows = out_ref.shape[0] // 2, out_ref.shape[1]
    width = out_ref.shape[2]
    share, half = width // NY, width // 2

    def tp_of(xx, zz, cc):
        return (xx * NZ + zz) * NC + cc

    def copy(src, dst, send, recv, r=None, t=None):
        return pltpu.make_async_remote_copy(
            src_ref=src, dst_ref=dst, send_sem=send, recv_sem=recv,
            device_id=(rep if r is None else r, tp if t is None else t),
            device_id_type=MESH,
        )

    sib = tp_of(x, zl, 1 - core)

    barrier = pltpu.get_barrier_semaphore()

    @pl.loop(1, tps)
    def _(j):
        pl.semaphore_signal(barrier, inc=1, device_id=(rep, (tp + j) % tps), device_id_type=MESH)

    @pl.loop(1, reps)
    def _(j):
        pl.semaphore_signal(barrier, inc=1, device_id=((rep + j) % reps, tp), device_id_type=MESH)

    def w_columns(d, q, cc):
        start = tp_of((x + d) % NX, q, cc) * width
        return w_ref.at[:, pl.ds(pl.multiple_of(start, width), width)]

    def way(q):
        return 1 if q < NZ // 2 else 3

    pairs = ((0, 3), (1, 2))
    order = []
    for pair in pairs:
        order += [(2, q) for q in pair] + [(NX - way(q), q) for q in pair]
    for pair in pairs:
        order += [(way(q), q) for q in pair]
    order += [(0, q) for pair in pairs for q in pair]
    x_load = pltpu.make_async_copy(x_hbm, x_ref, in_sem.at[0])
    x_load.start()
    tables = [
        pltpu.make_async_copy(src, dst, in_sem.at[i + 1])
        for i, (src, dst) in enumerate(
            ((adapter_h, adapter_s), (lengths_h, lengths_s), (target_h, target_s))
        )
    ]
    for c in tables:
        c.start()
    own_copies = {}
    for d, q in order:
        own_copies[d, q] = pltpu.make_async_copy(
            w_columns(d, q, core), w_own.at[d, q], w_own_sem.at[d, q]
        )
        own_copies[d, q].start()
    lib_copy = pltpu.make_async_copy(
        a_ref.at[pl.ds(pl.multiple_of(tp * width + y * share, share), share), :], lib.at[tp], lib_own
    )

    pl.semaphore_wait(barrier, tps - 1 + reps - 1)

    x_copy = copy(x_hbm, x_sib, x_send, x_recv, t=sib)
    x_copy.start()
    w_copies = {}
    for d, q in order:
        w_copies[d, q] = copy(
            w_columns(d, q, 1 - core), w_sib.at[d, q], w_send.at[d, q], w_recv.at[d, q], t=sib
        )

    def w_step(i):
        for key in order[4 * i:4 * i + 4]:
            w_copies[key].start()

    ready = set()

    def inputs(d, q):
        if not ready:
            x_load.wait()
            x_copy.wait_recv()
        if (d, q) not in ready:
            own_copies[d, q].wait()
            w_copies[d, q].wait_recv()
            ready.add((d, q))

    def partial(d, q, h=None):
        inputs(d, q)
        cols = slice(None) if h is None else pl.ds(h * half, half)
        return jnp.dot(x_ref[...], w_own[d, q, :, cols], preferred_element_type=F32) + jnp.dot(
            x_sib[...], w_sib[d, q, :, cols], preferred_element_type=F32
        )

    fars, dirs, accs, zs = {}, {}, {}, {}
    filled = set()

    def both_halves(buf, d, q):
        if (d, q) in filled:
            return
        filled.add((d, q))
        whole = partial(d, q).astype(BF)
        for h in range(2):
            buf[q, h] = whole[:, h * half:(h + 1) * half]

    def far_step(q, h):
        both_halves(s_far, 2, q)
        fars[q, h] = copy(
            s_far.at[q, h], r_far.at[q, h], far_send.at[q, h], far_recv.at[q, h],
            t=tp_of((x + way(q)) % NX, zl, core),
        )
        fars[q, h].start()

    def dir_step(q, h):
        d = NX - way(q)
        both_halves(s_dir, d, q)
        dirs[q, h] = copy(
            s_dir.at[q, h], r_dir.at[q, h], dir_send.at[q, h], dir_recv.at[q, h],
            t=tp_of((x + d) % NX, zl, core),
        )
        dirs[q, h].start()

    def acc_step(q, h):
        d = way(q)
        own = partial(d, q, h)
        fars[q, h].wait_recv()
        s_acc[q, h] = (own + r_far[q, h].astype(F32)).astype(BF)
        accs[q, h] = copy(
            s_acc.at[q, h], r_acc.at[q, h], acc_send.at[q, h], acc_recv.at[q, h],
            t=tp_of((x + d) % NX, zl, core),
        )
        accs[q, h].start()

    def z_step(q, h):
        own = partial(0, q, h)
        dirs[q, h].wait_recv()
        accs[q, h].wait_recv()
        total = own + r_dir[q, h].astype(F32) + r_acc[q, h].astype(F32)

        @pl.when(q == zl)
        def _():
            base[h] = total

        zs[q, h] = copy(
            s_z.at[q, h], r_z.at[zl, h], z_send.at[q, h], z_recv.at[zl, h], t=tp_of(x, q, core)
        )

        @pl.when(q != zl)
        def _():
            s_z[q, h] = total.astype(BF)
            zs[q, h].start()

    lib_all = copy(
        lib.at[pl.ds(0, tps - 1)], lib.at[pl.ds(0, tps - 1)], lib_send, lib_recv, t=sib
    )
    waits = []

    def lib_step():
        lib_copy.start()
        waits.append(lib_all)

        @pl.loop(1, tps)
        def _(j):
            to = (tp + j) % tps
            copy(
                a_ref.at[pl.ds(pl.multiple_of(to * width + y * share, share), share), :],
                lib.at[tp], lib_send, lib_recv, t=to,
            ).start()

    def choose_step():
        lib_copy.wait()
        lib_all.wait_recv()
        for j in range(1, NY):
            to = hi * NY + (y + j) % NY
            for p in range(prompts):
                s_sel[j, p] = lib[adapter_s[to * prompts + p]]
            c = copy(s_sel.at[j], sel.at[:, y], sel_send.at[j], sel_recv.at[y], r=to)
            c.start()
            waits.append(c)
        for p in range(prompts):
            sel[p, y] = lib[adapter_s[rep * prompts + p]]

    def chosen(p):
        return sel[p].reshape(width, sel.shape[3])

    rank = sel.shape[3] // 2
    thin = rows // NX
    line, place = NX * NC, x * NC + core

    def peer(j):
        other = (place + j) % line
        return other, tp_of(other // NC, zl, other % NC)

    def thin_rows(xx):
        return pl.ds(pl.multiple_of(xx * thin, thin), thin)

    def down_step():
        for j in range(1, NY):
            fr = (y + j) % NY
            copy(
                s_sel.at[j], sel.at[:, fr], sel_send.at[j], sel_recv.at[fr], r=hi * NY + fr
            ).wait_recv()
        for k in range(2):
            parts = [
                jnp.dot(
                    x_ref[pl.ds((2 * k + i) * rows, rows), :], chosen(2 * k + i),
                    preferred_element_type=F32,
                )
                for i in range(2)
            ]
            dpack[k] = jnp.concatenate([parts[0][:, :rank], parts[1][:, :rank]], axis=1)
        for j in range(1, line):
            other, to = peer(j)
            c = copy(
                dpack.at[other % NC, thin_rows(other // NC)], x_sum.at[place],
                down_send.at[j], down_recv.at[place], t=to,
            )
            c.start()
            waits.append(c)

    def down_z_step():
        total = dpack[core, thin_rows(x)]
        for j in range(1, line):
            other, to = peer(j)
            copy(
                dpack.at[core, thin_rows(x)], x_sum.at[other], down_send.at[j], down_recv.at[other], t=to
            ).wait_recv()
            total += x_sum[other]
        z_sum[zl] = total
        for j in range(1, NZ):
            c = copy(
                z_sum.at[zl], z_sum.at[zl], down_send.at[line + j], down_recv.at[line + zl],
                t=tp_of(x, (zl + j) % NZ, core),
            )
            c.start()
            waits.append(c)

    def down_back_step():
        for j in range(1, NZ):
            fr = (zl + j) % NZ
            copy(
                z_sum.at[fr], z_sum.at[fr], down_send.at[line + j], down_recv.at[line + fr],
                t=tp_of(x, fr, core),
            ).wait_recv()
        down[core, thin_rows(x)] = (z_sum[0] + z_sum[1]) + (z_sum[2] + z_sum[3])
        for j in range(1, line):
            other, to = peer(j)
            mine = down.at[core, thin_rows(x)]
            c = copy(
                mine, mine, down_send.at[line + NZ + j], down_recv.at[line + NZ + place], t=to
            )
            c.start()
            waits.append(c)

    def lift_step():
        for j in range(1, line):
            other, to = peer(j)
            theirs = down.at[other % NC, thin_rows(other // NC)]
            copy(
                theirs, theirs, down_send.at[line + NZ + j], down_recv.at[line + NZ + other], t=to
            ).wait_recv()
        lanes = lax.broadcasted_iota(jnp.int32, (rows, 2 * rank), 1)
        for p in range(prompts):
            pack = down[p // 2]
            if p % 2 == 0:
                pack = jnp.concatenate([pack[:, rank:], pack[:, :rank]], axis=1)
            pack = jnp.where(lanes >= rank, pack, 0.0).astype(BF)
            lift = 0.5 * lax.dot_general(
                pack, chosen(p), (((1,), (1,)), ((), ())), preferred_element_type=F32
            )
            for h in range(2):
                lifted[h, pl.ds(p * rows, rows), :] = lift[:, h * half:(h + 1) * half]

    outs = []

    def out_step(h):
        for j in range(1, NZ):
            fr = (zl + j) % NZ
            copy(
                s_z.at[0, h], r_z.at[fr, h], z_send.at[0, h], z_recv.at[fr, h], t=tp_of(x, fr, core)
            ).wait_recv()
        row_ids = lax.broadcasted_iota(jnp.int32, (rows, half), 0)
        results = []
        for p in range(prompts):
            span = pl.ds(p * rows, rows)
            total = base[h, span, :] + lifted[h, span, :]
            for j in range(1, NZ):
                total += r_z[(zl + j) % NZ, h, span, :].astype(F32)
            live = row_ids < lengths_s[rep * prompts + p]
            results.append(jnp.where(live, total, 0.0))
        cols = pl.ds(h * half, half)
        for j in FAR_FIRST:
            to = (rep + j) % reps
            value = jnp.zeros((rows, half), F32)
            for p in range(prompts):
                value = jnp.where(target_s[rep * prompts + p] == to, results[p], value)
            if j == 0:
                out_ref[rep, :, cols] = value.astype(BF)
            else:
                s_out[j, h] = value.astype(BF)
                c = copy(
                    s_out.at[j, h], out_ref.at[rep, :, cols], out_send.at[j, h], out_recv.at[rep, h], r=to
                )
                c.start()
                outs.append(c)

    for c in tables:
        c.wait()
    rounds = [(h, pair) for h in range(2) for pair in pairs]
    base_steps = {"F": far_step, "D": dir_step, "C": acc_step, "S": z_step}
    other_steps = {
        "lib": lib_step, "choose": choose_step, "down": down_step,
        "down_z": down_z_step, "down_back": down_back_step, "lift": lift_step,
    }
    for step in SCHEDULE:
        if step[0] == "W":
            w_step(int(step[1]))
        elif step[0] in base_steps:
            h, pair = rounds[int(step[1])]
            for q in pair:
                base_steps[step[0]](q, h)
        elif step[0] == "O":
            out_step(int(step[1]))
        else:
            other_steps[step]()

    x_copy.wait_send()
    for c in w_copies.values():
        c.wait_send()
    for group in (fars, dirs, accs):
        for c in group.values():
            c.wait_send()
    for q in range(NZ):
        @pl.when(q != zl)
        def _(q=q):
            for h in range(2):
                zs[q, h].wait_send()
    for c in waits + outs:
        c.wait_send()
    for h in range(2):
        for j in range(1, reps):
            fr = (rep + j) % reps
            copy(
                s_out.at[j, h], out_ref.at[fr, :, pl.ds(h * half, half)],
                out_send.at[j, h], out_recv.at[fr, h], r=fr,
            ).wait_recv()


def local(prompts, output_matrix, adapter_weight_pair, adapter, lengths, placement):
    count, rows, width = prompts.shape
    reps = lax.axis_size("rep")
    tps = lax.axis_size("tp")
    pair = adapter_weight_pair.shape[2]
    tall = count * rows
    dma = pltpu.SemaphoreType.DMA
    vmem = pl.BlockSpec(memory_space=pltpu.VMEM)
    hbm = pl.BlockSpec(memory_space=pltpu.HBM)
    table = pltpu.SMEM((adapter.shape[0],), jnp.int32)
    block = pltpu.VMEM((NZ, 2, tall, width // 2), BF)
    out = pl.pallas_call(
        kernel,
        out_shape=jax.ShapeDtypeStruct((reps, rows, width), BF),
        in_specs=[hbm] * 6,
        out_specs=vmem,
        scratch_shapes=[
            table, table, table,
            pltpu.VMEM((tall, width), BF),
            pltpu.VMEM((tall, width), BF),
            pltpu.VMEM((NX, NZ, width, width), BF),
            pltpu.VMEM((NX, NZ, width, width), BF),
            block, block, block, block, block, block,
            block, block, pltpu.VMEM((2, tall, width // 2), F32),
            pltpu.VMEM((tps, width // NY, pair), BF),
            pltpu.VMEM((NY, count, width // NY, pair), BF),
            pltpu.VMEM((count, NY, width // NY, pair), BF),
            pltpu.VMEM((2, rows, pair), F32),
            pltpu.VMEM((NX * NC, rows // NX, pair), F32),
            pltpu.VMEM((NZ, rows // NX, pair), F32),
            pltpu.VMEM((2, rows, pair), F32),
            pltpu.VMEM((2, tall, width // 2), F32),
            pltpu.VMEM((reps, 2, rows, width // 2), BF),
            dma((4,)), dma((NX, NZ)), dma((NX, NZ)), dma((NX, NZ)), dma, dma,
            dma((NZ, 2)), dma((NZ, 2)), dma((NZ, 2)), dma((NZ, 2)), dma((NZ, 2)), dma((NZ, 2)),
            dma((NZ, 2)), dma((NZ, 2)),
            dma, dma, dma, dma((NY,)), dma((NY,)),
            dma((2 * NX * NC + NZ,)), dma((2 * NX * NC + NZ,)), dma((reps, 2)), dma((reps, 2)),
        ],
        compiler_params=pltpu.CompilerParams(
            collective_id=0, has_side_effects=True, vmem_limit_bytes=60 * 1024 * 1024
        ),
    )(
        adapter, lengths, placement.reshape(-1), prompts.reshape(tall, width), output_matrix,
        adapter_weight_pair.reshape(-1, pair),
    )
    return out[None]


def solution(mesh):
    in_specs = (P("rep", None, "tp"), P("tp", None), P("tp", None, None), P(), P(), P())
    out_specs = P("rep", None, None, "tp")
    return jax.shard_map(local, mesh=mesh, in_specs=in_specs, out_specs=out_specs, check_vma=False)
```

time: 388 us -> 65.9 us (0.17); the launches traced: 384 us -> 65.5 us
  blocking collectives: 171 us -> 0 us
  waiting for transfers between devices: 82.2 us -> 0 us
  Pallas kernels: 0 us -> 63.7 us
  other arithmetic: 47 us -> 0 us
  local copies, waits for them, and re-layouts: 47.2 us -> 1.77 us
  matrix products: 16.3 us -> 0 us
  between operations: 13.5 us -> 0.01 us
  starting transfers between devices: 6.51 us -> 0 us
    psum x1 -> x0, blocking collectives: 144 us -> none  [local(): down_sum = lax.psum(down_part, 'tp').astype(jnp.bfloat16)]
    all_to_all x1 -> x0, waiting for transfers between devices: 82.1 us -> none  [local(): lax.all_to_all(adapter_weight_pair, 'tp', split_axis=1, concat_axis=0, ti...]
    pallas_call x0 -> x1, Pallas kernels: none -> 63.7 us  [local(): pl.pallas_call(kernel, out_shape=jax.ShapeDtypeStruct((reps, rows, width)...]
    unnamed x1 -> x0, other arithmetic: 45.2 us -> none
    unnamed x15 -> x1, local copies, waits for them, and re-layouts: 46.8 us -> 1.77 us
    all_to_all x1 -> x0, blocking collectives: 26.8 us -> none  [local(): lax.all_to_all(jnp.einsum('sj,jrf->srf', selector, prompts, preferred_ele...]
    dot_general x5 -> x0, matrix products: 16.3 us -> none  [the longest x1 12.2 us: local(): jnp.dot(received.reshape(item_count * row_count, received.shape[2]), outp...]
    all_to_all x1 -> x0, starting transfers between devices: 6.51 us -> none  [local(): lax.all_to_all(adapter_weight_pair, 'tp', split_axis=1, concat_axis=0, ti...]
  transfers between devices with their start and end apart: 2 -> 0, of which waited for: 1 -> 0; matrix products, arithmetic and copies ran while one was open for 24% -> 0% of each run, Pallas kernels for 0% -> 0%
where the time goes in v2:
time: 65.9 us; the launch traced here: 65.5 us
  Pallas kernels  63.7 us (97%)
  local copies, waits for them, and re-layouts  1.77 us (3%)
    pallas_call x1, Pallas kernels, local(): pl.pallas_call(kernel, out_shape=jax.ShapeDtypeStruct((reps, rows, width)...  63.7 us
    unnamed x1, local copies, waits for them, and re-layouts  1.77 us

profile of v2, /device:TPU:32, one launch (start us, length us, event | category | flops | bytes accessed | tf_op | source)
XLA Modules:
  0.0 65.5 jit_solution(13247493359863628890)
XLA Ops:
  0.0 63.7 %shard_map.64 = bf16[8,96,256]{2,1,0:T(8,128)(2,1)} custom-call(s32[32]{0:T(128)} %adapter_h.1, s32[32]{0:T(128)} %lengths_h.1, s32[32]{0:T(128)} %bitcast.7, bf16[384,256]{1,0:T(8,128)(2,1)} %bitcast.6, bf16[256,8192]{1,0:T(8,128)(2,1)} %w_ref.1, bf16[8192,128]{1,0:T(8,128)(2,1)} %bitcast.4), custom_call_target="tpu_custom_call" | custom-call | tf_op jit(solution)/shard_map/pallas_call | solution.py:400
  63.7 1.8 %copy.8 = bf16[1,8,96,256]{3,2,1,0:T(8,128)(2,1)} copy(bf16[1,8,96,256]{3,2,1,0:T(8,128)(2,1)} %bitcast.5) | data formatting | bytes 786432

commit v3 on v2

--- a/solution.py
+++ b/solution.py
@@ -13,10 +13,10 @@
 
 NX, NZ, NC = 4, 4, 2
 NY, NH = 4, 2
-FAR_FIRST = (6, 2, 5, 7, 4, 1, 3, 0)
+FAR_FIRST = (6, 5, 7, 4, 2, 1, 3, 0)
 SCHEDULE = (
     "W0", "lib", "F0", "W1", "W2", "W3", "D0", "C0", "F1", "D1", "S0", "C1", "choose", "F2",
-    "D2", "S1", "C2", "down", "F3", "D3", "S2", "down_z", "C3", "S3", "down_back", "lift", "O0", "O1",
+    "D2", "C2", "S1", "down", "F3", "D3", "S2", "down_z", "C3", "S3", "down_back", "lift", "O0", "O1",
 )
 
 
@@ -330,7 +330,7 @@
             results.append(jnp.where(live, total, 0.0))
         cols = pl.ds(h * half, half)
         for j in FAR_FIRST:
-            to = (rep + j) % reps
+            to = (hi + j // NY) % NH * NY + (y + j) % NY
             value = jnp.zeros((rows, half), F32)
             for p in range(prompts):
                 value = jnp.where(target_s[rep * prompts + p] == to, results[p], value)

time: 65.9 us -> 65.7 us (level)
  no operation moved by 1% of the time
where the time goes in v3:
time: 65.7 us; the launch traced here: 65.2 us
  Pallas kernels  63.5 us (97%)
  local copies, waits for them, and re-layouts  1.77 us (3%)
    pallas_call x1, Pallas kernels, local(): pl.pallas_call(kernel, out_shape=jax.ShapeDtypeStruct((reps, rows, width)...  63.5 us
    unnamed x1, local copies, waits for them, and re-layouts  1.77 us

profile of v3, /device:TPU:32, one launch (start us, length us, event | category | flops | bytes accessed | tf_op | source)
XLA Modules:
  0.0 65.2 jit_solution(6408673674449567319)
XLA Ops:
  0.0 63.5 %shard_map.64 = bf16[8,96,256]{2,1,0:T(8,128)(2,1)} custom-call(s32[32]{0:T(128)} %adapter_h.1, s32[32]{0:T(128)} %lengths_h.1, s32[32]{0:T(128)} %bitcast.7, bf16[384,256]{1,0:T(8,128)(2,1)} %bitcast.6, bf16[256,8192]{1,0:T(8,128)(2,1)} %w_ref.1, bf16[8192,128]{1,0:T(8,128)(2,1)} %bitcast.4), custom_call_target="tpu_custom_call" | custom-call | tf_op jit(solution)/shard_map/pallas_call | solution.py:400
  63.5 1.8 %copy.8 = bf16[1,8,96,256]{3,2,1,0:T(8,128)(2,1)} copy(bf16[1,8,96,256]{3,2,1,0:T(8,128)(2,1)} %bitcast.5) | data formatting | bytes 786432

commit v4 on v3

--- a/solution.py
+++ b/solution.py
@@ -311,7 +311,7 @@
             for h in range(2):
                 lifted[h, pl.ds(p * rows, rows), :] = lift[:, h * half:(h + 1) * half]
 
-    outs = []
+    outs, kept = [], []
 
     def out_step(h):
         for j in range(1, NZ):
@@ -335,7 +335,10 @@
             for p in range(prompts):
                 value = jnp.where(target_s[rep * prompts + p] == to, results[p], value)
             if j == 0:
-                out_ref[rep, :, cols] = value.astype(BF)
+                s_out[0, h] = value.astype(BF)
+                c = pltpu.make_async_copy(s_out.at[0, h], out_ref.at[rep, :, cols], out_send.at[0, h])
+                c.start()
+                kept.append(c)
             else:
                 s_out[j, h] = value.astype(BF)
                 c = copy(
@@ -377,6 +380,8 @@
                 zs[q, h].wait_send()
     for c in waits + outs:
         c.wait_send()
+    for c in kept:
+        c.wait()
     for h in range(2):
         for j in range(1, reps):
             fr = (rep + j) % reps
@@ -393,7 +398,6 @@
     pair = adapter_weight_pair.shape[2]
     tall = count * rows
     dma = pltpu.SemaphoreType.DMA
-    vmem = pl.BlockSpec(memory_space=pltpu.VMEM)
     hbm = pl.BlockSpec(memory_space=pltpu.HBM)
     table = pltpu.SMEM((adapter.shape[0],), jnp.int32)
     block = pltpu.VMEM((NZ, 2, tall, width // 2), BF)
@@ -401,7 +405,7 @@
         kernel,
         out_shape=jax.ShapeDtypeStruct((reps, rows, width), BF),
         in_specs=[hbm] * 6,
-        out_specs=vmem,
+        out_specs=hbm,
         scratch_shapes=[
             table, table, table,
             pltpu.VMEM((tall, width), BF),

time: 65.7 us -> 65 us (0.989)
  Pallas kernels: 63.5 us -> 62.8 us
    pallas_call x1, Pallas kernels: 63.5 us -> 62.8 us  [local(): pl.pallas_call(kernel, out_shape=jax.ShapeDtypeStruct((reps, rows, width)...]
where the time goes in v4:
time: 65 us; the launch traced here: 64.6 us
  Pallas kernels  62.8 us (97%)
  local copies, waits for them, and re-layouts  1.77 us (3%)
    pallas_call x1, Pallas kernels, local(): pl.pallas_call(kernel, out_shape=jax.ShapeDtypeStruct((reps, rows, width)...  62.8 us
    unnamed x1, local copies, waits for them, and re-layouts  1.77 us

profile of v4, /device:TPU:32, one launch (start us, length us, event | category | flops | bytes accessed | tf_op | source)
XLA Modules:
  0.0 64.6 jit_solution(9648597298827691032)
XLA Ops:
  0.0 62.8 %shard_map.64 = bf16[8,96,256]{2,1,0:T(8,128)(2,1)} custom-call(s32[32]{0:T(128)} %adapter_h.1, s32[32]{0:T(128)} %lengths_h.1, s32[32]{0:T(128)} %bitcast.7, bf16[384,256]{1,0:T(8,128)(2,1)} %bitcast.6, bf16[256,8192]{1,0:T(8,128)(2,1)} %w_ref.1, bf16[8192,128]{1,0:T(8,128)(2,1)} %bitcast.4), custom_call_target="tpu_custom_call" | custom-call | tf_op jit(solution)/shard_map/pallas_call | solution.py:404
  62.8 1.8 %copy.8 = bf16[1,8,96,256]{3,2,1,0:T(8,128)(2,1)} copy(bf16[1,8,96,256]{3,2,1,0:T(8,128)(2,1)} %bitcast.5) | data formatting | bytes 786432
